TPU v7x, 32 devices: a whole 2x2x4 slice. The times are simulated.
32 devices in a mesh: ha: 8 (over y, x, core), wa: 4 (over z).
Axes of the slice: x: 2, y: 2, z: 4, core: 2. Of those that a mesh axis runs over, the one named last changes fastest.
Arguments:
- token_queries: bfloat16 [16, 4, 32, 16, 128], P(None, None, 'ha', 'wa'), may hold values from -48 to 48
- token_keys: bfloat16 [16, 4, 32, 16, 128], P(None, None, 'ha', 'wa'), may hold values from -6 to 6
- token_values: bfloat16 [16, 4, 32, 16, 128], P(None, None, 'ha', 'wa'), may hold values from -6 to 6
Outputs:
- attended: bfloat16 [16, 4, 32, 16, 128], P(None, None, 'ha', 'wa')
All inputs are finite; a program needn't handle non-finite values.
Results may differ from a plain program's by a relative error of at most 0.0055.
Values may be sent and summed in bfloat16 or wider, within the bound.
A program may use at most 64 MiB of HBM per device.

v0:
```python
import jax
import jax.numpy as jnp
from jax import lax
from jax.sharding import PartitionSpec as P


def shifted(block, axis, distance):
    devices = range(lax.axis_size(axis))
    route = [((i - distance) % len(devices), i) for i in devices]
    return lax.ppermute(block, axis, route)


def fold_block(carry, queries, block_keys, block_values, factor):
    running_max, running_sum, weighted = carry
    scores = (
        jnp.einsum("hqd,hkd->hqk", queries, block_keys, preferred_element_type=jnp.float32) * factor
    )
    new_max = jnp.maximum(running_max, jnp.max(scores, axis=2))
    shrink = jnp.exp(running_max - new_max)
    weights = jnp.exp(scores - new_max[:, :, None])
    running_sum = running_sum * shrink + jnp.sum(weights, axis=2)
    mixed = jnp.einsum(
        "hqk,hkd->hqd",
        weights.astype(jnp.bfloat16),
        block_values,
        preferred_element_type=jnp.float32,
    )
    weighted = weighted * shrink[:, :, None] + mixed
    return (new_max, running_sum, weighted)


def cycle_attend(local_queries, local_keys, local_values, pass_keys, turns):
    head_local = local_queries.shape[0]
    head_size = local_queries.shape[-1]
    factor = head_size ** (-0.5)
    queries = local_queries.reshape(head_local, -1, head_size)
    key_rows = local_keys.reshape(head_local, -1, head_size)
    value_rows = local_values.reshape(head_local, -1, head_size)
    count = queries.shape[1]
    initial = (
        jnp.full((head_local, count), -1e30, jnp.float32),
        jnp.zeros((head_local, count), jnp.float32),
        jnp.zeros((head_local, count, head_size), jnp.float32),
    )
    first_state = fold_block(initial, queries, key_rows, value_rows, factor)

    def one_turn(turn_index, state):
        carry, moving_keys, moving_values = state
        moving_keys, moving_values = pass_keys(moving_keys, moving_values)
        carry = fold_block(carry, queries, moving_keys, moving_values, factor)
        return (carry, moving_keys, moving_values)

    final_state, spent_keys, spent_values = lax.fori_loop(
        0, turns, one_turn, (first_state, key_rows, value_rows)
    )
    result = final_state[2] / final_state[1][:, :, None]
    return result.astype(jnp.bfloat16).reshape(local_queries.shape)


def shards(token_queries, token_keys, token_values):
    local_queries, local_keys, local_values = (
        lax.all_to_all(token_queries, "wa", split_axis=0, concat_axis=3, tiled=True),
        lax.all_to_all(token_keys, "wa", split_axis=0, concat_axis=3, tiled=True),
        lax.all_to_all(token_values, "wa", split_axis=0, concat_axis=3, tiled=True),
    )

    def pass_height(moving_keys, moving_values):
        return shifted((moving_keys, moving_values), "ha", 1)

    local_out = cycle_attend(
        local_queries, local_keys, local_values, pass_height, lax.axis_size("ha") - 1
    )
    attended = lax.all_to_all(local_out, "wa", split_axis=3, concat_axis=0, tiled=True)
    return attended


def solution(mesh):
    placed = (
        P(None, None, "ha", "wa", None),
        P(None, None, "ha", "wa", None),
        P(None, None, "ha", "wa", None),
    )
    return jax.shard_map(
        shards,
        mesh=mesh,
        in_specs=placed,
        out_specs=P(None, None, "ha", "wa", None),
        check_vma=False,
    )
```

profile of v0, /device:TPU:0, one launch (start us, length us, event | category | flops | bytes accessed | tf_op | source)
XLA Modules:
  0.0 119.5 jit_solution(3771415241878944922)
XLA Ops:
  0.0 15.2 %all_to_all.63 = bf16[16,4,4,4,128]{4,3,2,1,0:T(4,128)(2,1)S(1)} all-to-all(bf16[16,4,4,4,128]{4,3,2,1,0:T(4,128)(2,1)} %param.5), channel_id=1, replica_groups=mesh['ha'=8,'wa'=4] {'wa'}, dimensions={0} | all-to-all | bytes 524288 | tf_op jit(solution)/shard_map/all_to_all | solution.py:62
  15.2 3.4 %all-to-all-start.1 = ((bf16[16,4,4,4,128]{4,3,2,1,0:T(4,128)(2,1)}), bf16[16,4,4,4,128]{4,3,2,1,0:T(4,128)(2,1)S(1)}, u32[]{:S(2)}, u32[]{:S(2)}) async-start(bf16[16,4,4,4,128]{4,3,2,1,0:T(4,128)(2,1)} %param.6), calls=%async_computation.1 | async-start | bytes 524288 | tf_op jit(solution)/shard_map/all_to_all | solution.py:63
  18.7 7.8 %all-to-all-done.1 = bf16[16,4,4,4,128]{4,3,2,1,0:T(4,128)(2,1)S(1)} async-done(((bf16[16,4,4,4,128]{4,3,2,1,0:T(4,128)(2,1)}), bf16[16,4,4,4,128]{4,3,2,1,0:T(4,128)(2,1)S(1)}, u32[]{:S(2)}, u32[]{:S(2)}) %all-to-all-start.1) | async-done | bytes 262176 | tf_op jit(solution)/shard_map/all_to_all | solution.py:63
  26.5 3.4 %all-to-all-start.2 = ((bf16[16,4,4,4,128]{4,3,2,1,0:T(4,128)(2,1)}), bf16[16,4,4,4,128]{4,3,2,1,0:T(4,128)(2,1)S(1)}, u32[]{:S(2)}, u32[]{:S(2)}) async-start(bf16[16,4,4,4,128]{4,3,2,1,0:T(4,128)(2,1)} %param.7), calls=%async_computation.2 | async-start | bytes 524288 | tf_op jit(solution)/shard_map/all_to_all | solution.py:64
  30.1 0.3 fusion.10
  30.4 0.2 fusion.5
  30.6 6.1 %all-to-all-done.2 = bf16[16,4,4,4,128]{4,3,2,1,0:T(4,128)(2,1)S(1)} async-done(((bf16[16,4,4,4,128]{4,3,2,1,0:T(4,128)(2,1)}), bf16[16,4,4,4,128]{4,3,2,1,0:T(4,128)(2,1)S(1)}, u32[]{:S(2)}, u32[]{:S(2)}) %all-to-all-start.2) | async-done | bytes 262176 | tf_op jit(solution)/shard_map/all_to_all | solution.py:64
  36.8 0.4 convolution_add_fusion.1
  37.2 70.4 %while.18 = (s32[]{:T(128)}, f32[4,256]{1,0:T(4,128)S(1)}, f32[4,256]{1,0:T(4,128)S(1)}, f32[4,256,128]{2,1,0:T(8,128)S(1)}, bf16[4,256,128]{2,1,0:T(8,128)(2,1)...) while((s32[]{:T(128)}, f32[4,256]{1,0:T(4,128)S(1)}, ...), condition=%wide.region_5.0_spmd, body=%wide.region_2.0_spmd.sunk | while | flops 136054784 | bytes 8192165 | solution.py:53
  37.3 1.6 %collective-permute-start.1 = (bf16[4,256,128]{2,1,0:T(8,128)(2,1)S(1)}, bf16[4,256,128]{2,1,0:T(8,128)(2,1)S(1)}, u32[]{:S(2)}, u32[]{:S(2)}) collective-permute-start(bf16[4,256,128]{2,1,0:T(8,128)(2,1)S(1)} %get-tuple-element.131), channel_id=1, source_target_pairs={{28,0},{0,4},{4,8},{8,12},{12,16},{16,20},{20,24},{24,28},{29,1},{... | collective-permute-start | bytes 786440 | tf_op jit(solution)/shard_map/while/body/eval_jaxpr/ppermute | solution.py:10
  38.9 5.1 %collective-permute-done = bf16[4,256,128]{2,1,0:T(8,128)(2,1)S(1)} collective-permute-done((bf16[4,256,128]{2,1,0:T(8,128)(2,1)S(1)}, bf16[4,256,128]{2,1,0:T(8,128)(2,1)S(1)}, u32[]{:S(2)}, u32[]{:S(2)}) %collective-permute-start) | collective-permute-done | bytes 262176 | tf_op jit(solution)/shard_map/while/body/eval_jaxpr/ppermute | solution.py:10
  44.0 0.3 fusion.27
  44.3 0.2 fusion.28
  44.5 2.3 %collective-permute-done.1 = bf16[4,256,128]{2,1,0:T(8,128)(2,1)S(1)} collective-permute-done((bf16[4,256,128]{2,1,0:T(8,128)(2,1)S(1)}, bf16[4,256,128]{2,1,0:T(8,128)(2,1)S(1)}, u32[]{:S(2)}, u32[]{:S(2)}) %collective-permute-start.1) | collective-permute-done | bytes 262176 | tf_op jit(solution)/shard_map/while/body/eval_jaxpr/ppermute | solution.py:10
  46.8 0.5 convolution_add_fusion.3
  47.3 0.7 collective-permute-start.1
  48.0 6.0 %collective-permute-done = bf16[4,256,128]{2,1,0:T(8,128)(2,1)S(1)} collective-permute-done((bf16[4,256,128]{2,1,0:T(8,128)(2,1)S(1)}, bf16[4,256,128]{2,1,0:T(8,128)(2,1)S(1)}, u32[]{:S(2)}, u32[]{:S(2)}) %collective-permute-start) | collective-permute-done | bytes 262176 | tf_op jit(solution)/shard_map/while/body/eval_jaxpr/ppermute | solution.py:10
  54.0 0.3 fusion.27
  54.6 2.3 %collective-permute-done.1 = bf16[4,256,128]{2,1,0:T(8,128)(2,1)S(1)} collective-permute-done((bf16[4,256,128]{2,1,0:T(8,128)(2,1)S(1)}, bf16[4,256,128]{2,1,0:T(8,128)(2,1)S(1)}, u32[]{:S(2)}, u32[]{:S(2)}) %collective-permute-start.1) | collective-permute-done | bytes 262176 | tf_op jit(solution)/shard_map/while/body/eval_jaxpr/ppermute | solution.py:10
  56.8 0.5 convolution_add_fusion.3
  57.5 6.6 %collective-permute-done = bf16[4,256,128]{2,1,0:T(8,128)(2,1)S(1)} collective-permute-done((bf16[4,256,128]{2,1,0:T(8,128)(2,1)S(1)}, bf16[4,256,128]{2,1,0:T(8,128)(2,1)S(1)}, u32[]{:S(2)}, u32[]{:S(2)}) %collective-permute-start) | collective-permute-done | bytes 262176 | tf_op jit(solution)/shard_map/while/body/eval_jaxpr/ppermute | solution.py:10
  64.1 0.3 fusion.27
  64.6 2.3 %collective-permute-done.1 = bf16[4,256,128]{2,1,0:T(8,128)(2,1)S(1)} collective-permute-done((bf16[4,256,128]{2,1,0:T(8,128)(2,1)S(1)}, bf16[4,256,128]{2,1,0:T(8,128)(2,1)S(1)}, u32[]{:S(2)}, u32[]{:S(2)}) %collective-permute-start.1) | collective-permute-done | bytes 262176 | tf_op jit(solution)/shard_map/while/body/eval_jaxpr/ppermute | solution.py:10
  66.9 0.5 convolution_add_fusion.3
  67.5 6.6 %collective-permute-done = bf16[4,256,128]{2,1,0:T(8,128)(2,1)S(1)} collective-permute-done((bf16[4,256,128]{2,1,0:T(8,128)(2,1)S(1)}, bf16[4,256,128]{2,1,0:T(8,128)(2,1)S(1)}, u32[]{:S(2)}, u32[]{:S(2)}) %collective-permute-start) | collective-permute-done | bytes 262176 | tf_op jit(solution)/shard_map/while/body/eval_jaxpr/ppermute | solution.py:10
  74.1 0.3 fusion.27
  74.5 0.2 fusion.28
  74.7 2.3 %collective-permute-done.1 = bf16[4,256,128]{2,1,0:T(8,128)(2,1)S(1)} collective-permute-done((bf16[4,256,128]{2,1,0:T(8,128)(2,1)S(1)}, bf16[4,256,128]{2,1,0:T(8,128)(2,1)S(1)}, u32[]{:S(2)}, u32[]{:S(2)}) %collective-permute-start.1) | collective-permute-done | bytes 262176 | tf_op jit(solution)/shard_map/while/body/eval_jaxpr/ppermute | solution.py:10
  77.0 0.5 convolution_add_fusion.3
  77.6 6.6 %collective-permute-done = bf16[4,256,128]{2,1,0:T(8,128)(2,1)S(1)} collective-permute-done((bf16[4,256,128]{2,1,0:T(8,128)(2,1)S(1)}, bf16[4,256,128]{2,1,0:T(8,128)(2,1)S(1)}, u32[]{:S(2)}, u32[]{:S(2)}) %collective-permute-start) | collective-permute-done | bytes 262176 | tf_op jit(solution)/shard_map/while/body/eval_jaxpr/ppermute | solution.py:10
  84.2 0.3 fusion.27
  84.5 0.2 fusion.28
  84.7 2.3 %collective-permute-done.1 = bf16[4,256,128]{2,1,0:T(8,128)(2,1)S(1)} collective-permute-done((bf16[4,256,128]{2,1,0:T(8,128)(2,1)S(1)}, bf16[4,256,128]{2,1,0:T(8,128)(2,1)S(1)}, u32[]{:S(2)}, u32[]{:S(2)}) %collective-permute-start.1) | collective-permute-done | bytes 262176 | tf_op jit(solution)/shard_map/while/body/eval_jaxpr/ppermute | solution.py:10
  87.0 0.5 convolution_add_fusion.3
  87.6 6.6 %collective-permute-done = bf16[4,256,128]{2,1,0:T(8,128)(2,1)S(1)} collective-permute-done((bf16[4,256,128]{2,1,0:T(8,128)(2,1)S(1)}, bf16[4,256,128]{2,1,0:T(8,128)(2,1)S(1)}, u32[]{:S(2)}, u32[]{:S(2)}) %collective-permute-start) | collective-permute-done | bytes 262176 | tf_op jit(solution)/shard_map/while/body/eval_jaxpr/ppermute | solution.py:10
  94.3 0.3 fusion.27
  94.8 2.3 %collective-permute-done.1 = bf16[4,256,128]{2,1,0:T(8,128)(2,1)S(1)} collective-permute-done((bf16[4,256,128]{2,1,0:T(8,128)(2,1)S(1)}, bf16[4,256,128]{2,1,0:T(8,128)(2,1)S(1)}, u32[]{:S(2)}, u32[]{:S(2)}) %collective-permute-start.1) | collective-permute-done | bytes 262176 | tf_op jit(solution)/shard_map/while/body/eval_jaxpr/ppermute | solution.py:10
  97.1 0.5 convolution_add_fusion.3
  97.7 6.6 %collective-permute-done = bf16[4,256,128]{2,1,0:T(8,128)(2,1)S(1)} collective-permute-done((bf16[4,256,128]{2,1,0:T(8,128)(2,1)S(1)}, bf16[4,256,128]{2,1,0:T(8,128)(2,1)S(1)}, u32[]{:S(2)}, u32[]{:S(2)}) %collective-permute-start) | collective-permute-done | bytes 262176 | tf_op jit(solution)/shard_map/while/body/eval_jaxpr/ppermute | solution.py:10
  104.3 0.3 fusion.27
  104.6 0.2 fusion.28
  104.9 2.3 %collective-permute-done.1 = bf16[4,256,128]{2,1,0:T(8,128)(2,1)S(1)} collective-permute-done((bf16[4,256,128]{2,1,0:T(8,128)(2,1)S(1)}, bf16[4,256,128]{2,1,0:T(8,128)(2,1)S(1)}, u32[]{:S(2)}, u32[]{:S(2)}) %collective-permute-start.1) | collective-permute-done | bytes 262176 | tf_op jit(solution)/shard_map/while/body/eval_jaxpr/ppermute | solution.py:10
  107.1 0.5 convolution_add_fusion.3
  107.6 0.2 divide_convert_fusion
  108.0 10.4 %all_to_all.64 = bf16[4,4,4,16,128]{4,2,1,0,3:T(4,128)(2,1)S(1)} all-to-all(bf16[4,4,4,16,128]{4,2,1,0,3:T(4,128)(2,1)S(1)} %copy.34), channel_id=1, replica_groups=mesh['ha'=8,'wa'=4] {'wa'}, dimensions={3} | all-to-all | bytes 524288 | tf_op jit(solution)/shard_map/all_to_all | solution.py:73
  118.3 0.2 copy.35
  118.5 0.2 copy.36
  118.7 0.8 copy.37
  (56 shorter events, 2.1 us)
Async XLA Ops:
  15.2 11.3 %all-to-all-start.1 = ((bf16[16,4,4,4,128]{4,3,2,1,0:T(4,128)(2,1)}), bf16[16,4,4,4,128]{4,3,2,1,0:T(4,128)(2,1)S(1)}, u32[]{:S(2)}, u32[]{:S(2)}) async-start(bf16[16,4,4,4,128]{4,3,2,1,0:T(4,128)(2,1)} %param.6), calls=%async_computation.1 | async-start | bytes 524288 | tf_op jit(solution)/shard_map/all_to_all | solution.py:63
  26.5 10.2 %all-to-all-start.2 = ((bf16[16,4,4,4,128]{4,3,2,1,0:T(4,128)(2,1)}), bf16[16,4,4,4,128]{4,3,2,1,0:T(4,128)(2,1)S(1)}, u32[]{:S(2)}, u32[]{:S(2)}) async-start(bf16[16,4,4,4,128]{4,3,2,1,0:T(4,128)(2,1)} %param.7), calls=%async_computation.2 | async-start | bytes 524288 | tf_op jit(solution)/shard_map/all_to_all | solution.py:64
  37.2 6.7 %collective-permute-start = (bf16[4,256,128]{2,1,0:T(8,128)(2,1)S(1)}, bf16[4,256,128]{2,1,0:T(8,128)(2,1)S(1)}, u32[]{:S(2)}, u32[]{:S(2)}) collective-permute-start(bf16[4,256,128]{2,1,0:T(8,128)(2,1)S(1)} %get-tuple-element.130), channel_id=1, source_target_pairs={{28,0},{0,4},{4,8},{8,12},{12,16},{16,20},{20,24},{24,28},{29,1},{... | collective-permute-start | bytes 786440 | tf_op jit(solution)/shard_map/while/body/eval_jaxpr/ppermute | solution.py:10
  37.3 9.5 %collective-permute-start.1 = (bf16[4,256,128]{2,1,0:T(8,128)(2,1)S(1)}, bf16[4,256,128]{2,1,0:T(8,128)(2,1)S(1)}, u32[]{:S(2)}, u32[]{:S(2)}) collective-permute-start(bf16[4,256,128]{2,1,0:T(8,128)(2,1)S(1)} %get-tuple-element.131), channel_id=1, source_target_pairs={{28,0},{0,4},{4,8},{8,12},{12,16},{16,20},{20,24},{24,28},{29,1},{... | collective-permute-start | bytes 786440 | tf_op jit(solution)/shard_map/while/body/eval_jaxpr/ppermute | solution.py:10
  47.3 6.7 %collective-permute-start = (bf16[4,256,128]{2,1,0:T(8,128)(2,1)S(1)}, bf16[4,256,128]{2,1,0:T(8,128)(2,1)S(1)}, u32[]{:S(2)}, u32[]{:S(2)}) collective-permute-start(bf16[4,256,128]{2,1,0:T(8,128)(2,1)S(1)} %get-tuple-element.130), channel_id=1, source_target_pairs={{28,0},{0,4},{4,8},{8,12},{12,16},{16,20},{20,24},{24,28},{29,1},{... | collective-permute-start | bytes 786440 | tf_op jit(solution)/shard_map/while/body/eval_jaxpr/ppermute | solution.py:10
  47.3 9.5 %collective-permute-start.1 = (bf16[4,256,128]{2,1,0:T(8,128)(2,1)S(1)}, bf16[4,256,128]{2,1,0:T(8,128)(2,1)S(1)}, u32[]{:S(2)}, u32[]{:S(2)}) collective-permute-start(bf16[4,256,128]{2,1,0:T(8,128)(2,1)S(1)} %get-tuple-element.131), channel_id=1, source_target_pairs={{28,0},{0,4},{4,8},{8,12},{12,16},{16,20},{20,24},{24,28},{29,1},{... | collective-permute-start | bytes 786440 | tf_op jit(solution)/shard_map/while/body/eval_jaxpr/ppermute | solution.py:10
  57.3 6.7 %collective-permute-start = (bf16[4,256,128]{2,1,0:T(8,128)(2,1)S(1)}, bf16[4,256,128]{2,1,0:T(8,128)(2,1)S(1)}, u32[]{:S(2)}, u32[]{:S(2)}) collective-permute-start(bf16[4,256,128]{2,1,0:T(8,128)(2,1)S(1)} %get-tuple-element.130), channel_id=1, source_target_pairs={{28,0},{0,4},{4,8},{8,12},{12,16},{16,20},{20,24},{24,28},{29,1},{... | collective-permute-start | bytes 786440 | tf_op jit(solution)/shard_map/while/body/eval_jaxpr/ppermute | solution.py:10
  57.4 9.5 %collective-permute-start.1 = (bf16[4,256,128]{2,1,0:T(8,128)(2,1)S(1)}, bf16[4,256,128]{2,1,0:T(8,128)(2,1)S(1)}, u32[]{:S(2)}, u32[]{:S(2)}) collective-permute-start(bf16[4,256,128]{2,1,0:T(8,128)(2,1)S(1)} %get-tuple-element.131), channel_id=1, source_target_pairs={{28,0},{0,4},{4,8},{8,12},{12,16},{16,20},{20,24},{24,28},{29,1},{... | collective-permute-start | bytes 786440 | tf_op jit(solution)/shard_map/while/body/eval_jaxpr/ppermute | solution.py:10
  67.4 6.7 %collective-permute-start = (bf16[4,256,128]{2,1,0:T(8,128)(2,1)S(1)}, bf16[4,256,128]{2,1,0:T(8,128)(2,1)S(1)}, u32[]{:S(2)}, u32[]{:S(2)}) collective-permute-start(bf16[4,256,128]{2,1,0:T(8,128)(2,1)S(1)} %get-tuple-element.130), channel_id=1, source_target_pairs={{28,0},{0,4},{4,8},{8,12},{12,16},{16,20},{20,24},{24,28},{29,1},{... | collective-permute-start | bytes 786440 | tf_op jit(solution)/shard_map/while/body/eval_jaxpr/ppermute | solution.py:10
  67.5 9.5 %collective-permute-start.1 = (bf16[4,256,128]{2,1,0:T(8,128)(2,1)S(1)}, bf16[4,256,128]{2,1,0:T(8,128)(2,1)S(1)}, u32[]{:S(2)}, u32[]{:S(2)}) collective-permute-start(bf16[4,256,128]{2,1,0:T(8,128)(2,1)S(1)} %get-tuple-element.131), channel_id=1, source_target_pairs={{28,0},{0,4},{4,8},{8,12},{12,16},{16,20},{20,24},{24,28},{29,1},{... | collective-permute-start | bytes 786440 | tf_op jit(solution)/shard_map/while/body/eval_jaxpr/ppermute | solution.py:10
  77.4 6.7 %collective-permute-start = (bf16[4,256,128]{2,1,0:T(8,128)(2,1)S(1)}, bf16[4,256,128]{2,1,0:T(8,128)(2,1)S(1)}, u32[]{:S(2)}, u32[]{:S(2)}) collective-permute-start(bf16[4,256,128]{2,1,0:T(8,128)(2,1)S(1)} %get-tuple-element.130), channel_id=1, source_target_pairs={{28,0},{0,4},{4,8},{8,12},{12,16},{16,20},{20,24},{24,28},{29,1},{... | collective-permute-start | bytes 786440 | tf_op jit(solution)/shard_map/while/body/eval_jaxpr/ppermute | solution.py:10
  77.5 9.5 %collective-permute-start.1 = (bf16[4,256,128]{2,1,0:T(8,128)(2,1)S(1)}, bf16[4,256,128]{2,1,0:T(8,128)(2,1)S(1)}, u32[]{:S(2)}, u32[]{:S(2)}) collective-permute-start(bf16[4,256,128]{2,1,0:T(8,128)(2,1)S(1)} %get-tuple-element.131), channel_id=1, source_target_pairs={{28,0},{0,4},{4,8},{8,12},{12,16},{16,20},{20,24},{24,28},{29,1},{... | collective-permute-start | bytes 786440 | tf_op jit(solution)/shard_map/while/body/eval_jaxpr/ppermute | solution.py:10
  87.5 6.7 %collective-permute-start = (bf16[4,256,128]{2,1,0:T(8,128)(2,1)S(1)}, bf16[4,256,128]{2,1,0:T(8,128)(2,1)S(1)}, u32[]{:S(2)}, u32[]{:S(2)}) collective-permute-start(bf16[4,256,128]{2,1,0:T(8,128)(2,1)S(1)} %get-tuple-element.130), channel_id=1, source_target_pairs={{28,0},{0,4},{4,8},{8,12},{12,16},{16,20},{20,24},{24,28},{29,1},{... | collective-permute-start | bytes 786440 | tf_op jit(solution)/shard_map/while/body/eval_jaxpr/ppermute | solution.py:10
  87.6 9.5 %collective-permute-start.1 = (bf16[4,256,128]{2,1,0:T(8,128)(2,1)S(1)}, bf16[4,256,128]{2,1,0:T(8,128)(2,1)S(1)}, u32[]{:S(2)}, u32[]{:S(2)}) collective-permute-start(bf16[4,256,128]{2,1,0:T(8,128)(2,1)S(1)} %get-tuple-element.131), channel_id=1, source_target_pairs={{28,0},{0,4},{4,8},{8,12},{12,16},{16,20},{20,24},{24,28},{29,1},{... | collective-permute-start | bytes 786440 | tf_op jit(solution)/shard_map/while/body/eval_jaxpr/ppermute | solution.py:10
  97.6 6.7 %collective-permute-start = (bf16[4,256,128]{2,1,0:T(8,128)(2,1)S(1)}, bf16[4,256,128]{2,1,0:T(8,128)(2,1)S(1)}, u32[]{:S(2)}, u32[]{:S(2)}) collective-permute-start(bf16[4,256,128]{2,1,0:T(8,128)(2,1)S(1)} %get-tuple-element.130), channel_id=1, source_target_pairs={{28,0},{0,4},{4,8},{8,12},{12,16},{16,20},{20,24},{24,28},{29,1},{... | collective-permute-start | bytes 786440 | tf_op jit(solution)/shard_map/while/body/eval_jaxpr/ppermute | solution.py:10
  97.6 9.5 %collective-permute-start.1 = (bf16[4,256,128]{2,1,0:T(8,128)(2,1)S(1)}, bf16[4,256,128]{2,1,0:T(8,128)(2,1)S(1)}, u32[]{:S(2)}, u32[]{:S(2)}) collective-permute-start(bf16[4,256,128]{2,1,0:T(8,128)(2,1)S(1)} %get-tuple-element.131), channel_id=1, source_target_pairs={{28,0},{0,4},{4,8},{8,12},{12,16},{16,20},{20,24},{24,28},{29,1},{... | collective-permute-start | bytes 786440 | tf_op jit(solution)/shard_map/while/body/eval_jaxpr/ppermute | solution.py:10
where the time goes:
time: 120 us
  waiting for transfers between devices  73.9 us (62%)
  blocking collectives  25.6 us (21%)
  starting transfers between devices  9.8 us (8%)
  matrix products  6.07 us (5%)
  local copies, waits for them, and re-layouts  1.96 us (2%)
  other arithmetic  1.67 us (1%)
    ppermute x14, waiting for transfers between devices, shifted(): return lax.ppermute(block, axis, route)  60 us
    all_to_all x1, blocking collectives, shards(): lax.all_to_all(token_queries, 'wa', split_axis=0, concat_axis=3, tiled=True)  15.2 us
    all_to_all x1, blocking collectives, shards(): lax.all_to_all(local_out, 'wa', split_axis=3, concat_axis=0, tiled=True)  10.4 us
    all_to_all x1, waiting for transfers between devices, shards(): lax.all_to_all(token_keys, 'wa', split_axis=0, concat_axis=3, tiled=True)  7.78 us
    all_to_all x1, waiting for transfers between devices, shards(): lax.all_to_all(token_values, 'wa', split_axis=0, concat_axis=3, tiled=True)  6.11 us
    dot_general x8, matrix products, fold_block(): jnp.einsum('hqk,hkd->hqd', weights.astype(jnp.bfloat16), block_values, pr...  3.59 us
    all_to_all x1, starting transfers between devices, shards(): lax.all_to_all(token_values, 'wa', split_axis=0, concat_axis=3, tiled=True)  3.41 us
    all_to_all x1, starting transfers between devices, shards(): lax.all_to_all(token_keys, 'wa', split_axis=0, concat_axis=3, tiled=True)  3.41 us
  transfers between devices with their start and end apart: 16, of which 16 were waited for; matrix products, arithmetic and copies ran while one was open for 4% of the time, Pallas kernels for 0%

commit v1 on v0

v1 whole, which is shorter than its diff:
```python
import functools

import jax
import jax.numpy as jnp
from jax import lax
from jax.experimental import pallas as pl
from jax.experimental.pallas import tpu as pltpu
from jax.sharding import PartitionSpec as P

MESH = pl.DeviceIdType.MESH
LOG2E = 1.4426950408889634
KEY_TILE = 2048
SLOTS_AT_ONCE = 4


def slot_order(subgroups, width):
    def rank(offset):
        up, across = offset
        distance = min(across, width - across)
        return (-distance, up == 0, across, up)

    return sorted(((u, w) for u in range(subgroups) for w in range(width)), key=rank)


def attend(queries, keys, values, key_count, factor):
    tile = min(KEY_TILE, key_count)
    scale = factor * LOG2E

    def scores_of(index):
        return lax.dot_general(
            queries, keys(index, tile), (((1,), (1,)), ((), ())), preferred_element_type=jnp.float32
        )

    def mix(weights, index):
        return jnp.dot(
            weights.astype(jnp.bfloat16), values(index, tile), preferred_element_type=jnp.float32
        )

    scores = scores_of(0)
    top = jnp.max(scores, axis=1, keepdims=True)
    weights = jnp.exp2((scores - top) * scale)
    total = jnp.sum(weights, axis=1, keepdims=True)
    mixed = mix(weights, 0)

    def fold(index, state):
        top, total, mixed = state
        scores = scores_of(index)
        new_top = jnp.maximum(top, jnp.max(scores, axis=1, keepdims=True))
        shrink = jnp.exp2((top - new_top) * scale)
        weights = jnp.exp2((scores - new_top) * scale)
        total = total * shrink + jnp.sum(weights, axis=1, keepdims=True)
        return new_top, total, mixed * shrink + mix(weights, index)

    if key_count > tile:
        top, total, mixed = lax.fori_loop(1, key_count // tile, fold, (top, total, mixed))
    return (mixed / total).astype(jnp.bfloat16)


def kernel(
    height, width, group, q_ref, k_ref, v_ref, o_ref, qb, kb, vb, ob,
    send_sem, recv_sem, pass_send, pass_recv,
):
    subgroups = height // group
    order = slot_order(subgroups, width)
    slots = len(order)
    own = slots - 1
    length, size = k_ref.shape[1], k_ref.shape[2]
    factor = size ** (-0.5)
    ha, wa = lax.axis_index("ha"), lax.axis_index("wa")
    member, sub = lax.rem(ha, group), lax.div(ha, group)

    def peer(slot, sign):
        up, across = order[slot]
        to_sub = lax.rem(sub + (up if sign > 0 else subgroups - up), subgroups)
        to_wa = lax.rem(wa + (across if sign > 0 else width - across), width)
        return (to_sub * group + member, to_wa), to_sub * width + to_wa

    def sibling(step):
        return (sub * group + lax.rem(member + step, group), wa)

    def each_sibling(act):
        if group == 2:
            act(1)
        elif group > 2:
            pl.loop(1, group)(act)

    my_head = sub * width + wa

    barrier = pltpu.get_barrier_semaphore()
    for slot in range(own):
        pl.semaphore_signal(barrier, inc=1, device_id=peer(slot, 1)[0], device_id_type=MESH)
    each_sibling(
        lambda step: pl.semaphore_signal(
            barrier, inc=1, device_id=sibling(step), device_id_type=MESH
        )
    )
    own_copies = [
        pltpu.make_async_copy(src.at[my_head], dst, recv_sem.at[t, own])
        for t, (src, dst) in enumerate(
            ((k_ref, kb.at[0, own]), (v_ref, vb.at[0, own]), (q_ref, qb.at[own]))
        )
    ]
    for copy in own_copies:
        copy.start()
    pl.semaphore_wait(barrier, own + group - 1)

    def to_peer(t, slot):
        src, dst = ((k_ref, kb.at[0, slot]), (v_ref, vb.at[0, slot]), (q_ref, qb.at[slot]))[t]
        device, head = peer(slot, 1)
        return pltpu.make_async_remote_copy(
            src_ref=src.at[head],
            dst_ref=dst,
            send_sem=send_sem.at[t, slot],
            recv_sem=recv_sem.at[t, slot],
            device_id=device,
            device_id_type=MESH,
        )

    sent = [[to_peer(t, slot) for slot in range(own)] for t in range(3)]
    for row in sent:
        for copy in row:
            copy.start()

    def to_sibling(t, slot, step):
        buf = (kb, vb)[t]
        return pltpu.make_async_remote_copy(
            src_ref=buf.at[0, slot],
            dst_ref=buf.at[step, slot],
            send_sem=pass_send.at[t, step - 1],
            recv_sem=pass_recv.at[t, step - 1],
            device_id=sibling(step),
            device_id_type=MESH,
        )

    for t in range(2):
        for slot in (own, *range(own)):
            if slot == own:
                own_copies[t].wait()
            else:
                sent[t][slot].wait_recv()
            each_sibling(lambda step: to_sibling(t, slot, step).start())

    def whole_pass(t, step):
        buf = (kb, vb)[t]
        return pltpu.make_async_remote_copy(
            src_ref=buf.at[0],
            dst_ref=buf.at[step],
            send_sem=pass_send.at[t, step - 1],
            recv_sem=pass_recv.at[t, step - 1],
            device_id=sibling(step),
            device_id_type=MESH,
        )

    for t in range(2):
        each_sibling(lambda step: whole_pass(t, step).wait_recv())

    key_count = group * slots * length

    def tile_of(buf):
        def read(index, tile):
            if tile == key_count:
                return buf[...].reshape(key_count, size)
            blocks = tile // length
            per = slots // blocks
            if per == 0:
                rows = blocks // slots
                return buf[pl.ds(index * rows, rows)].reshape(tile, size)
            first = lax.rem(index, per) * blocks
            return buf[lax.div(index, per), pl.ds(first, blocks)].reshape(tile, size)

        return read

    returned = []
    for first in range(0, slots, SLOTS_AT_ONCE):
        here = range(first, min(first + SLOTS_AT_ONCE, slots))
        for slot in here:
            if slot == own:
                own_copies[2].wait()
            else:
                sent[2][slot].wait_recv()
        rows = len(here) * length
        result = attend(
            qb[first : first + len(here)].reshape(rows, size),
            tile_of(kb),
            tile_of(vb),
            key_count,
            factor,
        )
        ob[first : first + len(here)] = result.reshape(len(here), length, size)
        for slot in here:
            if slot == own:
                copy = pltpu.make_async_copy(ob.at[own], o_ref.at[my_head], recv_sem.at[3, own])
            else:
                copy = pltpu.make_async_remote_copy(
                    src_ref=ob.at[slot],
                    dst_ref=o_ref.at[my_head],
                    send_sem=send_sem.at[3, slot],
                    recv_sem=recv_sem.at[3, slot],
                    device_id=peer(slot, -1)[0],
                    device_id_type=MESH,
                )
            copy.start()
            returned.append(copy)

    for t in range(2):
        each_sibling(lambda step: whole_pass(t, step).wait_send())
    for row in sent:
        for copy in row:
            copy.wait_send()
    for slot in range(slots):
        returned[slot].wait()


def shards(height, width, token_queries, token_keys, token_values):
    heads, size = token_queries.shape[0], token_queries.shape[-1]
    group = height * width // heads
    blocks = [x.reshape(heads, -1, size) for x in (token_queries, token_keys, token_values)]
    length = blocks[0].shape[1]
    slots = (height // group) * width
    kind = token_queries.dtype
    count = group * slots * length
    pairs = slots * length * count * heads // slots
    out = pl.pallas_call(
        functools.partial(kernel, height, width, group),
        out_shape=jax.ShapeDtypeStruct(blocks[0].shape, kind),
        in_specs=[pl.BlockSpec(memory_space=pl.ANY)] * 3,
        out_specs=pl.BlockSpec(memory_space=pl.ANY),
        scratch_shapes=[
            pltpu.VMEM((slots, length, size), kind),
            pltpu.VMEM((group, slots, length, size), kind),
            pltpu.VMEM((group, slots, length, size), kind),
            pltpu.VMEM((slots, length, size), kind),
            pltpu.SemaphoreType.DMA((4, slots)),
            pltpu.SemaphoreType.DMA((4, slots)),
            pltpu.SemaphoreType.DMA((2, max(group - 1, 1))),
            pltpu.SemaphoreType.DMA((2, max(group - 1, 1))),
        ],
        compiler_params=pltpu.CompilerParams(
            collective_id=0, has_side_effects=True, vmem_limit_bytes=56 * 2**20
        ),
        cost_estimate=pl.CostEstimate(
            flops=4 * pairs * size, bytes_accessed=8 * heads * length * size, transcendentals=pairs
        ),
        name="attention_exchange",
    )(*blocks)
    return out.reshape(token_queries.shape)


def solution(mesh):
    height, width = mesh.shape["ha"], mesh.shape["wa"]
    placed = P(None, None, "ha", "wa", None)
    return jax.shard_map(
        functools.partial(shards, height, width),
        mesh=mesh,
        in_specs=(placed, placed, placed),
        out_specs=placed,
        check_vma=False,
    )
```

time: 120 us -> 36.6 us (0.30)
  waiting for transfers between devices: 73.9 us -> 0 us
  Pallas kernels: 0 us -> 34.7 us
  blocking collectives: 25.6 us -> 0 us
  starting transfers between devices: 9.8 us -> 0 us
  matrix products: 6.07 us -> 0 us
  other arithmetic: 1.67 us -> 0 us
    ppermute x14 -> x0, waiting for transfers between devices: 60 us -> none  [shifted(): return lax.ppermute(block, axis, route)]
    pallas_call x0 -> x1, Pallas kernels: none -> 34.7 us  [shards(): pl.pallas_call(functools.partial(kernel, height, width, group), out_shape...]
    all_to_all x2 -> x0, blocking collectives: 25.6 us -> none  [the longest x1 15.2 us: shards(): lax.all_to_all(token_queries, 'wa', split_axis=0, concat_axis=3, tiled=True)]
    all_to_all x2 -> x0, waiting for transfers between devices: 13.9 us -> none  [the longest x1 7.78 us: shards(): lax.all_to_all(token_keys, 'wa', split_axis=0, concat_axis=3, tiled=True)]
    all_to_all x2 -> x0, starting transfers between devices: 6.82 us -> none  [the longest x1 3.41 us: shards(): lax.all_to_all(token_values, 'wa', split_axis=0, concat_axis=3, tiled=True)]
    dot_general x16 -> x0, matrix products: 6.07 us -> none  [the longest x8 3.59 us: fold_block(): jnp.einsum('hqk,hkd->hqd', weights.astype(jnp.bfloat16), block_values, pr...]
    ppermute x14 -> x0, starting transfers between devices: 2.98 us -> none  [shifted(): return lax.ppermute(block, axis, route)]
    unnamed x0 -> x1, local copies, waits for them, and re-layouts: none -> 1.76 us
  transfers between devices with their start and end apart: 16 -> 0, of which waited for: 16 -> 0; matrix products, arithmetic and copies ran while one was open for 4% -> 0% of each run, Pallas kernels for 0% -> 0%
where the time goes in v1:
time: 36.6 us; the launch traced here: 36.4 us
  Pallas kernels  34.7 us (95%)
  local copies, waits for them, and re-layouts  1.76 us (5%)
    pallas_call x1, Pallas kernels, shards(): pl.pallas_call(functools.partial(kernel, height, width, group), out_shape...  34.7 us
    unnamed x1, local copies, waits for them, and re-layouts  1.76 us

profile of v1, /device:TPU:0, one launch (start us, length us, event | category | flops | bytes accessed | tf_op | source)
XLA Modules:
  0.0 36.4 jit_solution(2220826446522606519)
XLA Ops:
  0.0 34.7 %attention_exchange.1 = bf16[16,64,128]{2,1,0:T(8,128)(2,1)} custom-call(bf16[16,64,128]{2,1,0:T(8,128)(2,1)} %bitcast.5, bf16[16,64,128]{2,1,0:T(8,128)(2,1)} %bitcast.6, bf16[16,64,128]{2,1,0:T(8,128)(2,1)} %bitcast.7), custom_call_target="tpu_custom_call" | custom-call | flops 1073741824 | bytes 1048576 | tf_op jit(solution)/shard_map/attention_exchange/pallas_call | solution.py:223
  34.7 1.8 %copy.5 = bf16[16,4,4,4,128]{4,3,2,1,0:T(4,128)(2,1)} copy(bf16[16,4,4,4,128]{4,3,2,1,0:T(4,128)(2,1)} %bitcast.4) | data formatting | bytes 524288

commit v2 on v1

--- a/solution.py
+++ b/solution.py
@@ -1,4 +1,5 @@
 import functools
+import math
 
 import jax
 import jax.numpy as jnp
@@ -117,8 +118,8 @@
         )
 
     sent = [[to_peer(t, slot) for slot in range(own)] for t in range(3)]
-    for row in sent:
-        for copy in row:
+    for t in range(2):
+        for copy in sent[t]:
             copy.start()
 
     def to_sibling(t, slot, step):
@@ -139,6 +140,9 @@
             else:
                 sent[t][slot].wait_recv()
             each_sibling(lambda step: to_sibling(t, slot, step).start())
+            if t == 1 and slot != own:
+                sent[1][slot].wait_send()
+                sent[2][slot].start()
 
     def whole_pass(t, step):
         buf = (kb, vb)[t]
@@ -204,11 +208,26 @@
 
     for t in range(2):
         each_sibling(lambda step: whole_pass(t, step).wait_send())
-    for row in sent:
-        for copy in row:
+    for t in (0, 2):
+        for copy in sent[t]:
             copy.wait_send()
     for slot in range(slots):
         returned[slot].wait()
+
+
+def hand_over(src_ref, dst_ref, sem):
+    parts = sem.shape[0]
+    rows = src_ref.shape[0] // parts
+    copies = [
+        pltpu.make_async_copy(
+            src_ref.at[pl.ds(i * rows, rows)], dst_ref.at[pl.ds(i * rows, rows)], sem.at[i]
+        )
+        for i in range(parts)
+    ]
+    for copy in copies:
+        copy.start()
+    for copy in copies:
+        copy.wait()
 
 
 def shards(height, width, token_queries, token_keys, token_values):
@@ -243,6 +262,17 @@
         ),
         name="attention_exchange",
     )(*blocks)
+    out = pl.pallas_call(
+        hand_over,
+        out_shape=jax.ShapeDtypeStruct(out.shape, kind),
+        in_specs=[pl.BlockSpec(memory_space=pl.ANY)],
+        out_specs=pl.BlockSpec(memory_space=pl.ANY),
+        scratch_shapes=[pltpu.SemaphoreType.DMA((math.gcd(heads, 4),))],
+        cost_estimate=pl.CostEstimate(
+            flops=0, bytes_accessed=4 * heads * length * size, transcendentals=0
+        ),
+        name="hand_over",
+    )(out)
     return out.reshape(token_queries.shape)
 
 

time: 36.6 us -> 43.4 us (1.19)
  Pallas kernels: 34.7 us -> 43.2 us
  local copies, waits for them, and re-layouts: 1.76 us -> 0 us
    pallas_call x0 -> x1, Pallas kernels: none -> 9.08 us  [shards(): pl.pallas_call(hand_over, out_shape=jax.ShapeDtypeStruct(out.shape, kind)...]
    unnamed x1 -> x0, local copies, waits for them, and re-layouts: 1.76 us -> none
    pallas_call x1, Pallas kernels: 34.7 us -> 34.1 us  [shards(): pl.pallas_call(functools.partial(kernel, height, width, group), out_shape...]
where the time goes in v2:
time: 43.4 us; the launch traced here: 43.2 us
  Pallas kernels  43.2 us (100%)
    pallas_call x1, Pallas kernels, shards(): pl.pallas_call(functools.partial(kernel, height, width, group), out_shape...  34.1 us
    pallas_call x1, Pallas kernels, shards(): pl.pallas_call(hand_over, out_shape=jax.ShapeDtypeStruct(out.shape, kind)...  9.08 us

profile of v2, /device:TPU:0, one launch (start us, length us, event | category | flops | bytes accessed | tf_op | source)
XLA Modules:
  0.0 43.2 jit_solution(1275912173834188622)
XLA Ops:
  0.0 34.1 %attention_exchange.1.src_ref = bf16[16,64,128]{2,1,0:T(8,128)(2,1)} custom-call(bf16[16,64,128]{2,1,0:T(8,128)(2,1)} %bitcast.4, bf16[16,64,128]{2,1,0:T(8,128)(2,1)} %bitcast.5, bf16[16,64,128]{2,1,0:T(8,128)(2,1)} %bitcast.6), custom_call_target="tpu_custom_call" | custom-call | flops 1073741824 | bytes 1048576 | tf_op jit(solution)/shard_map/attention_exchange/pallas_call | solution.py:242
  34.2 9.1 %hand_over.1 = bf16[16,64,128]{2,1,0:T(8,128)(2,1)} custom-call(bf16[16,64,128]{2,1,0:T(8,128)(2,1)} %attention_exchange.1.src_ref), custom_call_target="tpu_custom_call" | custom-call | bytes 524288 | tf_op jit(solution)/shard_map/hand_over/pallas_call | solution.py:265

commit v3 on v2

--- a/solution.py
+++ b/solution.py
@@ -1,5 +1,4 @@
 import functools
-import math
 
 import jax
 import jax.numpy as jnp
@@ -59,7 +58,7 @@
 
 def kernel(
     height, width, group, q_ref, k_ref, v_ref, o_ref, qb, kb, vb, ob,
-    send_sem, recv_sem, pass_send, pass_recv,
+    send_sem, recv_sem, pass_send, pass_recv, ready,
 ):
     subgroups = height // group
     order = slot_order(subgroups, width)
@@ -90,11 +89,18 @@
     barrier = pltpu.get_barrier_semaphore()
     for slot in range(own):
         pl.semaphore_signal(barrier, inc=1, device_id=peer(slot, 1)[0], device_id_type=MESH)
-    each_sibling(
-        lambda step: pl.semaphore_signal(
-            barrier, inc=1, device_id=sibling(step), device_id_type=MESH
-        )
-    )
+
+    def tell_later(step):
+        @pl.when(member + step < group)
+        def _():
+            pl.semaphore_signal(barrier, inc=1, device_id=sibling(step), device_id_type=MESH)
+
+    def tell_earlier(step):
+        @pl.when(member + step >= group)
+        def _():
+            pl.semaphore_signal(ready, inc=1, device_id=sibling(step), device_id_type=MESH)
+
+    each_sibling(tell_later)
     own_copies = [
         pltpu.make_async_copy(src.at[my_head], dst, recv_sem.at[t, own])
         for t, (src, dst) in enumerate(
@@ -103,7 +109,7 @@
     ]
     for copy in own_copies:
         copy.start()
-    pl.semaphore_wait(barrier, own + group - 1)
+    pl.semaphore_wait(barrier, own + member)
 
     def to_peer(t, slot):
         src, dst = ((k_ref, kb.at[0, slot]), (v_ref, vb.at[0, slot]), (q_ref, qb.at[slot]))[t]
@@ -121,6 +127,12 @@
     for t in range(2):
         for copy in sent[t]:
             copy.start()
+    each_sibling(tell_earlier)
+
+    @pl.when(member + 1 < group)
+    def _():
+        pl.semaphore_wait(ready, group - 1 - member)
+
 
     def to_sibling(t, slot, step):
         buf = (kb, vb)[t]
@@ -215,19 +227,8 @@
         returned[slot].wait()
 
 
-def hand_over(src_ref, dst_ref, sem):
-    parts = sem.shape[0]
-    rows = src_ref.shape[0] // parts
-    copies = [
-        pltpu.make_async_copy(
-            src_ref.at[pl.ds(i * rows, rows)], dst_ref.at[pl.ds(i * rows, rows)], sem.at[i]
-        )
-        for i in range(parts)
-    ]
-    for copy in copies:
-        copy.start()
-    for copy in copies:
-        copy.wait()
+def hand_over(src_ref, dst_ref):
+    dst_ref[...] = src_ref[...]
 
 
 def shards(height, width, token_queries, token_keys, token_values):
@@ -253,6 +254,7 @@
             pltpu.SemaphoreType.DMA((4, slots)),
             pltpu.SemaphoreType.DMA((2, max(group - 1, 1))),
             pltpu.SemaphoreType.DMA((2, max(group - 1, 1))),
+            pltpu.SemaphoreType.REGULAR,
         ],
         compiler_params=pltpu.CompilerParams(
             collective_id=0, has_side_effects=True, vmem_limit_bytes=56 * 2**20
@@ -265,9 +267,8 @@
     out = pl.pallas_call(
         hand_over,
         out_shape=jax.ShapeDtypeStruct(out.shape, kind),
-        in_specs=[pl.BlockSpec(memory_space=pl.ANY)],
-        out_specs=pl.BlockSpec(memory_space=pl.ANY),
-        scratch_shapes=[pltpu.SemaphoreType.DMA((math.gcd(heads, 4),))],
+        in_specs=[pl.BlockSpec(memory_space=pltpu.VMEM)],
+        out_specs=pl.BlockSpec(memory_space=pltpu.VMEM),
         cost_estimate=pl.CostEstimate(
             flops=0, bytes_accessed=4 * heads * length * size, transcendentals=0
         ),

time: 43.4 us -> 36 us (0.83)
  Pallas kernels: 43.2 us -> 35.8 us
    pallas_call x1, Pallas kernels: 9.08 us -> 1.67 us  [shards(): pl.pallas_call(hand_over, out_shape=jax.ShapeDtypeStruct(out.shape, kind)...]
where the time goes in v3:
time: 36 us; the launch traced here: 35.8 us
  Pallas kernels  35.8 us (99%)
    pallas_call x1, Pallas kernels, shards(): pl.pallas_call(functools.partial(kernel, height, width, group), out_shape...  34.2 us
    pallas_call x1, Pallas kernels, shards(): pl.pallas_call(hand_over, out_shape=jax.ShapeDtypeStruct(out.shape, kind)...  1.67 us

profile of v3, /device:TPU:0, one launch (start us, length us, event | category | flops | bytes accessed | tf_op | source)
XLA Modules:
  0.0 35.8 jit_solution(8246243838303328120)
XLA Ops:
  0.0 34.2 %attention_exchange.1.src_ref = bf16[16,64,128]{2,1,0:T(8,128)(2,1)} custom-call(bf16[16,64,128]{2,1,0:T(8,128)(2,1)} %bitcast.4, bf16[16,64,128]{2,1,0:T(8,128)(2,1)} %bitcast.5, bf16[16,64,128]{2,1,0:T(8,128)(2,1)} %bitcast.6), custom_call_target="tpu_custom_call" | custom-call | flops 1073741824 | bytes 1048576 | tf_op jit(solution)/shard_map/attention_exchange/pallas_call | solution.py:243
  34.2 1.7 %hand_over.1 = bf16[16,64,128]{2,1,0:T(8,128)(2,1)} custom-call(bf16[16,64,128]{2,1,0:T(8,128)(2,1)} %attention_exchange.1.src_ref), custom_call_target="tpu_custom_call" | custom-call | bytes 524288 | tf_op jit(solution)/shard_map/hand_over/pallas_call | solution.py:267

commit v4 on v3

--- a/solution.py
+++ b/solution.py
@@ -127,6 +127,12 @@
     for t in range(2):
         for copy in sent[t]:
             copy.start()
+
+    @pl.when(member == 0)
+    def _():
+        for copy in sent[2]:
+            copy.start()
+
     each_sibling(tell_earlier)
 
     @pl.when(member + 1 < group)
@@ -154,7 +160,7 @@
             each_sibling(lambda step: to_sibling(t, slot, step).start())
             if t == 1 and slot != own:
                 sent[1][slot].wait_send()
-                sent[2][slot].start()
+                pl.when(member > 0)(sent[2][slot].start)
 
     def whole_pass(t, step):
         buf = (kb, vb)[t]

time: 36 us -> 35.6 us (0.989)
  Pallas kernels: 35.8 us -> 35.4 us
    pallas_call x1, Pallas kernels: 34.2 us -> 33.8 us  [shards(): pl.pallas_call(functools.partial(kernel, height, width, group), out_shape...]
where the time goes in v4:
time: 35.6 us; the launch traced here: 35.5 us
  Pallas kernels  35.4 us (99%)
    pallas_call x1, Pallas kernels, shards(): pl.pallas_call(functools.partial(kernel, height, width, group), out_shape...  33.8 us
    pallas_call x1, Pallas kernels, shards(): pl.pallas_call(hand_over, out_shape=jax.ShapeDtypeStruct(out.shape, kind)...  1.67 us

profile of v4, /device:TPU:0, one launch (start us, length us, event | category | flops | bytes accessed | tf_op | source)
XLA Modules:
  0.0 35.5 jit_solution(9356735481070963296)
XLA Ops:
  0.0 33.8 %attention_exchange.1.src_ref = bf16[16,64,128]{2,1,0:T(8,128)(2,1)} custom-call(bf16[16,64,128]{2,1,0:T(8,128)(2,1)} %bitcast.4, bf16[16,64,128]{2,1,0:T(8,128)(2,1)} %bitcast.5, bf16[16,64,128]{2,1,0:T(8,128)(2,1)} %bitcast.6), custom_call_target="tpu_custom_call" | custom-call | flops 1073741824 | bytes 1048576 | tf_op jit(solution)/shard_map/attention_exchange/pallas_call | solution.py:249
  33.8 1.7 %hand_over.1 = bf16[16,64,128]{2,1,0:T(8,128)(2,1)} custom-call(bf16[16,64,128]{2,1,0:T(8,128)(2,1)} %attention_exchange.1.src_ref), custom_call_target="tpu_custom_call" | custom-call | bytes 524288 | tf_op jit(solution)/shard_map/hand_over/pallas_call | solution.py:273

commit v5 on v4

--- a/solution.py
+++ b/solution.py
@@ -58,7 +58,7 @@
 
 def kernel(
     height, width, group, q_ref, k_ref, v_ref, o_ref, qb, kb, vb, ob,
-    send_sem, recv_sem, pass_send, pass_recv, ready,
+    send_sem, recv_sem, pass_send, pass_recv, ready, here,
 ):
     subgroups = height // group
     order = slot_order(subgroups, width)
@@ -86,9 +86,20 @@
 
     my_head = sub * width + wa
 
+    place = wa * subgroups + sub
+
+    def is_before(slot):
+        (to_ha, to_wa), _ = peer(slot, 1)
+        return to_wa * subgroups + lax.div(to_ha, group) < place
+
+    before = [is_before(slot) for slot in range(own)]
     barrier = pltpu.get_barrier_semaphore()
+
+    def tell_peer(slot, semaphore):
+        pl.semaphore_signal(semaphore, inc=1, device_id=peer(slot, 1)[0], device_id_type=MESH)
+
     for slot in range(own):
-        pl.semaphore_signal(barrier, inc=1, device_id=peer(slot, 1)[0], device_id_type=MESH)
+        pl.when(~before[slot])(functools.partial(tell_peer, slot, barrier))
 
     def tell_later(step):
         @pl.when(member + step < group)
@@ -109,7 +120,15 @@
     ]
     for copy in own_copies:
         copy.start()
-    pl.semaphore_wait(barrier, own + member)
+
+    @pl.when(place + member > 0)
+    def _():
+        pl.semaphore_wait(barrier, place + member)
+
+    for slot in range(own):
+        up, across = order[slot]
+        back = order.index(((subgroups - up) % subgroups, (width - across) % width))
+        pl.when(before[slot])(functools.partial(tell_peer, slot, here.at[back]))
 
     def to_peer(t, slot):
         src, dst = ((k_ref, kb.at[0, slot]), (v_ref, vb.at[0, slot]), (q_ref, qb.at[slot]))[t]
@@ -125,8 +144,16 @@
 
     sent = [[to_peer(t, slot) for slot in range(own)] for t in range(3)]
     for t in range(2):
-        for copy in sent[t]:
-            copy.start()
+        for slot in range(own):
+            pl.when(before[slot])(sent[t][slot].start)
+    for t in range(2):
+        for slot in range(own):
+
+            @pl.when(~before[slot])
+            def _():
+                if t == 0:
+                    pl.semaphore_wait(here.at[slot], 1)
+                sent[t][slot].start()
 
     @pl.when(member == 0)
     def _():
@@ -194,22 +221,22 @@
 
     returned = []
     for first in range(0, slots, SLOTS_AT_ONCE):
-        here = range(first, min(first + SLOTS_AT_ONCE, slots))
-        for slot in here:
+        chunk = range(first, min(first + SLOTS_AT_ONCE, slots))
+        for slot in chunk:
             if slot == own:
                 own_copies[2].wait()
             else:
                 sent[2][slot].wait_recv()
-        rows = len(here) * length
+        rows = len(chunk) * length
         result = attend(
-            qb[first : first + len(here)].reshape(rows, size),
+            qb[first : first + len(chunk)].reshape(rows, size),
             tile_of(kb),
             tile_of(vb),
             key_count,
             factor,
         )
-        ob[first : first + len(here)] = result.reshape(len(here), length, size)
-        for slot in here:
+        ob[first : first + len(chunk)] = result.reshape(len(chunk), length, size)
+        for slot in chunk:
             if slot == own:
                 copy = pltpu.make_async_copy(ob.at[own], o_ref.at[my_head], recv_sem.at[3, own])
             else:
@@ -261,6 +288,7 @@
             pltpu.SemaphoreType.DMA((2, max(group - 1, 1))),
             pltpu.SemaphoreType.DMA((2, max(group - 1, 1))),
             pltpu.SemaphoreType.REGULAR,
+            pltpu.SemaphoreType.REGULAR((slots,)),
         ],
         compiler_params=pltpu.CompilerParams(
             collective_id=0, has_side_effects=True, vmem_limit_bytes=56 * 2**20

time: 35.6 us -> 38.3 us (1.076)
  Pallas kernels: 35.4 us -> 38.1 us
    pallas_call x1, Pallas kernels: 33.8 us -> 36.4 us  [shards(): pl.pallas_call(functools.partial(kernel, height, width, group), out_shape...]
where the time goes in v5:
time: 38.3 us; the launch traced here: 38.1 us
  Pallas kernels  38.1 us (99%)
    pallas_call x1, Pallas kernels, shards(): pl.pallas_call(functools.partial(kernel, height, width, group), out_shape...  36.4 us
    pallas_call x1, Pallas kernels, shards(): pl.pallas_call(hand_over, out_shape=jax.ShapeDtypeStruct(out.shape, kind)...  1.67 us

profile of v5, /device:TPU:0, one launch (start us, length us, event | category | flops | bytes accessed | tf_op | source)
XLA Modules:
  0.0 38.1 jit_solution(18439849623542175171)
XLA Ops:
  0.0 36.4 %attention_exchange.1.src_ref = bf16[16,64,128]{2,1,0:T(8,128)(2,1)} custom-call(bf16[16,64,128]{2,1,0:T(8,128)(2,1)} %bitcast.4, bf16[16,64,128]{2,1,0:T(8,128)(2,1)} %bitcast.5, bf16[16,64,128]{2,1,0:T(8,128)(2,1)} %bitcast.6), custom_call_target="tpu_custom_call" | custom-call | flops 1073741824 | bytes 1048576 | tf_op jit(solution)/shard_map/attention_exchange/pallas_call | solution.py:276
  36.4 1.7 %hand_over.1 = bf16[16,64,128]{2,1,0:T(8,128)(2,1)} custom-call(bf16[16,64,128]{2,1,0:T(8,128)(2,1)} %attention_exchange.1.src_ref), custom_call_target="tpu_custom_call" | custom-call | bytes 524288 | tf_op jit(solution)/shard_map/hand_over/pallas_call | solution.py:301

commit v6 on v4

--- a/solution.py
+++ b/solution.py
@@ -13,13 +13,27 @@
 SLOTS_AT_ONCE = 4
 
 
+def swaps(count):
+    return count & (count - 1) == 0
+
+
 def slot_order(subgroups, width):
     def rank(offset):
         up, across = offset
-        distance = min(across, width - across)
-        return (-distance, up == 0, across, up)
+        far = across.bit_length() if swaps(width) else min(across, width - across)
+        return (-far, up == 0, up, across)
 
     return sorted(((u, w) for u in range(subgroups) for w in range(width)), key=rank)
+
+
+def partner(index, offset, count, sign):
+    if not swaps(count):
+        return lax.rem(index + (offset if sign > 0 else count - offset), count)
+    for bit in range(offset.bit_length()):
+        step = 1 << bit
+        if offset & step:
+            index = index + step - 2 * step * lax.rem(lax.div(index, step), 2)
+    return index
 
 
 def attend(queries, keys, values, key_count, factor):
@@ -71,8 +85,8 @@
 
     def peer(slot, sign):
         up, across = order[slot]
-        to_sub = lax.rem(sub + (up if sign > 0 else subgroups - up), subgroups)
-        to_wa = lax.rem(wa + (across if sign > 0 else width - across), width)
+        to_sub = partner(sub, up, subgroups, sign)
+        to_wa = partner(wa, across, width, sign)
         return (to_sub * group + member, to_wa), to_sub * width + to_wa
 
     def sibling(step):

time: 35.6 us -> 35.3 us (level)
  no operation moved by 1% of the time
where the time goes in v6:
time: 35.3 us; the launch traced here: 35.1 us
  Pallas kernels  35.1 us (99%)
    pallas_call x1, Pallas kernels, shards(): pl.pallas_call(functools.partial(kernel, height, width, group), out_shape...  33.4 us
    pallas_call x1, Pallas kernels, shards(): pl.pallas_call(hand_over, out_shape=jax.ShapeDtypeStruct(out.shape, kind)...  1.67 us

profile of v6, /device:TPU:0, one launch (start us, length us, event | category | flops | bytes accessed | tf_op | source)
XLA Modules:
  0.0 35.1 jit_solution(2848522411011625844)
XLA Ops:
  0.0 33.4 %attention_exchange.1.src_ref = bf16[16,64,128]{2,1,0:T(8,128)(2,1)} custom-call(bf16[16,64,128]{2,1,0:T(8,128)(2,1)} %bitcast.4, bf16[16,64,128]{2,1,0:T(8,128)(2,1)} %bitcast.5, bf16[16,64,128]{2,1,0:T(8,128)(2,1)} %bitcast.6), custom_call_target="tpu_custom_call" | custom-call | flops 1073741824 | bytes 1048576 | tf_op jit(solution)/shard_map/attention_exchange/pallas_call | solution.py:263
  33.4 1.7 %hand_over.1 = bf16[16,64,128]{2,1,0:T(8,128)(2,1)} custom-call(bf16[16,64,128]{2,1,0:T(8,128)(2,1)} %attention_exchange.1.src_ref), custom_call_target="tpu_custom_call" | custom-call | bytes 524288 | tf_op jit(solution)/shard_map/hand_over/pallas_call | solution.py:287
